TPU v7x, 256 devices: a whole 4x4x8 slice. The times are simulated.
256 devices in a mesh: ctx: 16 (over y, x), exp: 16 (over z, core).
Axes of the slice: x: 4, y: 4, z: 8, core: 2. Of those that a mesh axis runs over, the one named last changes fastest.
Arguments:
- tokens: bfloat16 [32768, 2048], P(('ctx', 'exp')), may hold values from -6 to 6
- expert_ids: int32 [32768, 8], P(('ctx', 'exp')), may hold values from 0 to 127, all different within a row; in each aligned block of 128 rows (0 to 127, 128 to 255, ...) at most 10 rows name the same one
- gate_probs: float32 [32768, 8], P(('ctx', 'exp')), may hold values from 0.05 to 1
- w_gate: bfloat16 [256, 2048, 384], P(('ctx', 'exp')), may hold values from -0.125 to 0.125
- w_up: bfloat16 [256, 2048, 384], P(('ctx', 'exp')), may hold values from -0.125 to 0.125
- w_down: bfloat16 [256, 384, 2048], P(('ctx', 'exp')), may hold values from -0.21875 to 0.21875
Outputs:
- mixed: bfloat16 [32768, 2048], P(('ctx', 'exp'))
Inputs may be any that keep to these rules, and one draw needn't show every extreme that they name: `expert_ids`: each row names 8 different experts. Among the 128 rows of one device no expert is named by more than 10 rows, a bound that some block reaches.
All inputs are finite; a program needn't handle non-finite values.
Results may differ from a plain program's by a relative error of at most 0.0065.
Values may be sent and summed in bfloat16 or wider, within the bound.
A program may use at most 128 MiB of HBM per device.

v0:
```python
import jax
import jax.numpy as jnp
from jax import lax
from jax.sharding import PartitionSpec as P


def expert_half(row_block, gate_half, up_half, down_half):
    gate_sum = jnp.dot(row_block, gate_half, preferred_element_type=jnp.float32)
    up_sum = jnp.dot(row_block, up_half, preferred_element_type=jnp.float32)
    hidden = (jax.nn.silu(gate_sum) * up_sum).astype(jnp.bfloat16)
    return jnp.dot(hidden, down_half, preferred_element_type=jnp.float32).astype(jnp.bfloat16)


def shards(tokens, expert_ids, gate_probs, w_gate, w_up, w_down):
    tok_rows, features = tokens.shape
    chosen = expert_ids.shape[1]
    ctx_size = lax.axis_size("ctx")
    exp_size = lax.axis_size("exp")
    groups = exp_size // 2
    experts = ctx_size * groups
    capacity = 2 * max(1, tok_rows * chosen * 5 // (8 * experts))
    flat_ids = expert_ids.reshape(-1)
    matches = (flat_ids[:, None] == jnp.arange(experts, dtype=jnp.int32)[None, :]).astype(jnp.int32)
    slot_rank = jnp.sum((jnp.cumsum(matches, axis=0) - matches) * matches, axis=1)
    places = flat_ids * capacity + slot_rank
    owners = (
        jnp.full((experts * capacity,), tok_rows, jnp.int32)
        .at[places]
        .set(jnp.arange(tok_rows * chosen, dtype=jnp.int32) // chosen)
    )
    padded = jnp.concatenate([tokens, jnp.zeros((1, features), tokens.dtype)], axis=0)
    outgoing = padded[owners].reshape(ctx_size, groups, capacity, features)
    relayed = lax.all_to_all(outgoing, "ctx", split_axis=0, concat_axis=0, tiled=True)
    own_half = (w_gate[0], w_up[0], w_down[0])
    sendable = jnp.broadcast_to(
        relayed[:, :, None], (ctx_size, groups, 2, capacity, features)
    ).reshape(ctx_size, exp_size, capacity, features)
    halves = (own_half,)
    arrived = lax.all_to_all(sendable, "exp", split_axis=1, concat_axis=1, tiled=True)
    flat_rows = arrived.reshape(-1, features)
    result = expert_half(flat_rows, halves[0][0], halves[0][1], halves[0][2])
    returned = lax.all_to_all(
        result.reshape(arrived.shape), "exp", split_axis=1, concat_axis=1, tiled=True
    )
    combined = jnp.sum(
        returned.reshape(ctx_size, groups, 2, capacity, features).astype(jnp.float32), axis=2
    ).astype(jnp.bfloat16)
    homebound = lax.all_to_all(combined, "ctx", split_axis=0, concat_axis=0, tiled=True).reshape(
        experts * capacity, features
    )
    picked = homebound[places].reshape(tok_rows, chosen, features)
    weights = gate_probs / jnp.sum(gate_probs, axis=1, keepdims=True)
    mixed = jnp.sum(weights[:, :, None] * picked.astype(jnp.float32), axis=1)
    return mixed.astype(jnp.bfloat16)


def solution(mesh):
    return jax.shard_map(
        shards,
        mesh=mesh,
        in_specs=(
            P(("ctx", "exp"), None),
            P(("ctx", "exp"), None),
            P(("ctx", "exp"), None),
            P(("ctx", "exp"), None, None),
            P(("ctx", "exp"), None, None),
            P(("ctx", "exp"), None, None),
        ),
        out_specs=P(("ctx", "exp"), None),
        check_vma=False,
    )
```

profile of v0, /device:TPU:32, one launch (start us, length us, event | category | flops | bytes accessed | tf_op | source)
XLA Modules:
  0.0 822.2 jit_solution(3730566271419460380)
XLA Ops:
  0.0 0.0 copy-start
  0.0 0.9 copy.27
  0.9 0.1 eq.29
  1.0 0.1 eq.25
  1.1 0.7 broadcast_multiply_fusion
  1.8 0.1 copy.29
  1.9 0.2 fusion.10
  2.2 0.1 copy.30
  2.3 0.1 copy.26
  2.4 0.1 mul.37
  2.5 0.4 fusion.9
  2.9 4.3 scatter_custom_fusion
  7.2 1.1 concatenate.3
  8.3 6.3 gather_fusion
  14.6 9.5 %reshape.71 = bf16[16,8,10,2048]{3,2,1,0:T(8,128)(2,1)} reshape(bf16[1280,2048]{1,0:T(8,128)(2,1)} %gather_fusion) | data formatting | bytes 10485760 | tf_op jit(solution)/shard_map/reshape | solution.py:32
  24.1 6.8 copy.31
  30.9 68.9 %all_to_all.20 = bf16[16,8,10,2048]{3,1,2,0:T(8,128)(2,1)S(1)} all-to-all(bf16[16,8,10,2048]{3,1,2,0:T(8,128)(2,1)S(1)} %copy.31), channel_id=1, replica_groups=mesh['ctx'=16,'exp'=16] {'ctx'}, dimensions={0} | all-to-all | bytes 10485760 | tf_op jit(solution)/shard_map/all_to_all | solution.py:33
  99.8 5.2 copy.32
  105.1 8.2 %broadcast_in_dim.8 = bf16[16,8,2,10,2048]{4,0,3,2,1:T(8,128)(2,1)} broadcast(bf16[16,8,10,2048]{3,0,2,1:T(8,128)(2,1)} %copy.32), dimensions={0,1,3,4} | broadcast | bytes 15728640 | tf_op jit(solution)/shard_map/broadcast_in_dim | solution.py:35
  113.3 237.0 %all_to_all.21 = bf16[16,16,10,2048]{3,0,2,1:T(8,128)(2,1)S(1)} all-to-all(bf16[16,16,10,2048]{3,0,2,1:T(8,128)(2,1)} %bitcast.30), channel_id=1, replica_groups=mesh['ctx'=16,'exp'=16] {'exp'}, dimensions={1} | all-to-all | bytes 20971520 | tf_op jit(solution)/shard_map/all_to_all | solution.py:39
  350.3 21.2 %copy.33 = bf16[16,16,10,2048]{3,2,1,0:T(8,128)(2,1)} copy(bf16[16,16,10,2048]{3,0,2,1:T(8,128)(2,1)S(1)} %all_to_all.21) | data formatting | bytes 20971520 | tf_op jit(solution)/shard_map/all_to_all | solution.py:39
  371.4 18.1 %reshape.73 = bf16[2560,2048]{1,0:T(8,128)(2,1)} reshape(bf16[16,16,10,2048]{3,2,1,0:T(8,128)(2,1)} %copy.33) | data formatting | bytes 20971520 | tf_op jit(solution)/shard_map/reshape | solution.py:40
  389.5 10.0 %fusion.6 = f32[2560,384]{1,0:T(8,128)} fusion(bf16[2560,2048]{1,0:T(8,128)(2,1)} %reshape.73, bf16[1,2048,384]{2,1,0:T(8,128)(2,1)} %param.9), kind=kOutput, calls=%fused_computation.12 | convolution fusion | flops 4026531840 | bytes 15990784 | tf_op jit(solution)/shard_map/dot_general | solution.py:8
  399.5 0.0 copy-done
  399.6 17.3 %convolution_convert_fusion = bf16[2560,2048]{1,0:T(8,128)(2,1)} fusion(bf16[2560,2048]{1,0:T(8,128)(2,1)} %reshape.73, f32[2560,384]{1,0:T(8,128)} %fusion.6, bf16[1,384,2048]{2,1,0:T(8,128)(2,1)S(1)} %copy-done, bf16[1,2048,384]{2,1,0:T(8,128)(2,1)} %param.10), kind=kOutput, calls=%fused_computation.3 | convolution fusion | flops 8064204800 | bytes 28049408 | tf_op jit(solution)/shard_map/dot_general | solution.py:11
  416.9 17.6 %reshape.74 = bf16[16,16,10,2048]{3,2,1,0:T(8,128)(2,1)} reshape(bf16[2560,2048]{1,0:T(8,128)(2,1)} %convolution_convert_fusion) | data formatting | bytes 20971520 | tf_op jit(solution)/shard_map/reshape | solution.py:43
  434.5 10.7 %copy.34 = bf16[16,16,10,2048]{3,0,2,1:T(8,128)(2,1)S(1)} copy(bf16[16,16,10,2048]{3,2,1,0:T(8,128)(2,1)} %reshape.74) | data formatting | bytes 20971520 | tf_op jit(solution)/shard_map/reshape | solution.py:43
  445.2 234.0 %all_to_all.22 = bf16[16,16,10,2048]{3,0,2,1:T(8,128)(2,1)} all-to-all(bf16[16,16,10,2048]{3,0,2,1:T(8,128)(2,1)S(1)} %copy.34), channel_id=1, replica_groups=mesh['ctx'=16,'exp'=16] {'exp'}, dimensions={1} | all-to-all | bytes 20971520 | tf_op jit(solution)/shard_map/all_to_all | solution.py:42
  679.2 11.1 %bitcast_reduce_fusion = bf16[16,8,10,2048]{3,0,2,1:T(8,128)(2,1)} fusion(bf16[16,16,10,2048]{3,0,2,1:T(8,128)(2,1)} %all_to_all.22), kind=kLoop, calls=%fused_computation.4 | loop fusion | flops 2621440 | bytes 15728640 | tf_op jit(solution)/shard_map/reduce_sum | solution.py:45
  690.3 7.7 copy.35
  697.9 0.0 copy-start.2
  697.9 5.0 all-to-all-start.3
  702.9 0.0 copy-done.2
  702.9 0.1 copy.25
  703.0 79.3 %all-to-all-done.3 = bf16[16,8,10,2048]{3,1,2,0:T(8,128)(2,1)} async-done(((bf16[16,8,10,2048]{3,1,2,0:T(8,128)(2,1)}), bf16[16,8,10,2048]{3,1,2,0:T(8,128)(2,1)}, u32[]{:S(2)}, u32[]{:S(2)}) %all-to-all-start.3) | async-done | bytes 5242912 | tf_op jit(solution)/shard_map/all_to_all | solution.py:48
  782.3 10.4 %copy.36 = bf16[16,8,10,2048]{3,2,1,0:T(8,128)(2,1)} copy(bf16[16,8,10,2048]{3,1,2,0:T(8,128)(2,1)} %all-to-all-done.3) | data formatting | bytes 10485760 | tf_op jit(solution)/shard_map/all_to_all | solution.py:48
  792.7 9.8 %reshape.76 = bf16[1280,2048]{1,0:T(8,128)(2,1)} reshape(bf16[16,8,10,2048]{3,2,1,0:T(8,128)(2,1)} %copy.36) | data formatting | bytes 10485760 | tf_op jit(solution)/shard_map/reshape | solution.py:48
  802.5 0.0 copy-start.1
  802.5 12.1 %gather_fusion.1 = bf16[1024,2048]{1,0:T(8,128)(2,1)} fusion(bf16[1280,2048]{1,0:T(8,128)(2,1)} %reshape.76, s32[1024]{0:T(1024)S(1)} %broadcast_clamp_fusion), kind=kCustom, calls=%fused_computation.1 | custom fusion | bytes 8392704 | tf_op jit(solution)/shard_map/gather | solution.py:51
  814.6 7.3 fusion
  822.0 0.0 copy-done.1
  (11 shorter events, 0.1 us)
Async XLA Ops:
  0.0 399.5 %copy-start = (bf16[1,384,2048]{2,1,0:T(8,128)(2,1)S(1)}, bf16[1,384,2048]{2,1,0:T(8,128)(2,1)}, u32[]{:S(2)}) copy-start(bf16[1,384,2048]{2,1,0:T(8,128)(2,1)} %param.11) | copy-start | bytes 4718596
  697.9 5.0 copy-start.2
  697.9 84.4 %all-to-all-start.3 = ((bf16[16,8,10,2048]{3,1,2,0:T(8,128)(2,1)}), bf16[16,8,10,2048]{3,1,2,0:T(8,128)(2,1)}, u32[]{:S(2)}, u32[]{:S(2)}) async-start(bf16[16,8,10,2048]{3,1,2,0:T(8,128)(2,1)} %copy.35), calls=%async_computation.3 | async-start | bytes 10485760 | tf_op jit(solution)/shard_map/all_to_all | solution.py:48
  802.5 19.4 %copy-start.1 = (bf16[1,384,2048]{2,1,0:T(8,128)(2,1)S(1)}, bf16[1,384,2048]{2,1,0:T(8,128)(2,1)}, u32[]{:S(2)}) copy-start(bf16[1,384,2048]{2,1,0:T(8,128)(2,1)} %param.11) | copy-start | bytes 4718596
where the time goes:
time: 836 us; the launch traced here: 822 us
  blocking collectives  540 us (65%)
  local copies, waits for them, and re-layouts  151 us (18%)
  waiting for transfers between devices  79.3 us (9%)
  matrix products  27.3 us (3%)
  other arithmetic  19.8 us (2%)
    all_to_all x1, blocking collectives, shards(): lax.all_to_all(sendable, 'exp', split_axis=1, concat_axis=1, tiled=True)  237 us
    all_to_all x1, blocking collectives, shards(): lax.all_to_all(result.reshape(arrived.shape), 'exp', split_axis=1, concat...  234 us
    all_to_all x1, waiting for transfers between devices, shards(): lax.all_to_all(combined, 'ctx', split_axis=0, concat_axis=0, tiled=True)  79.3 us
    all_to_all x1, blocking collectives, shards(): lax.all_to_all(outgoing, 'ctx', split_axis=0, concat_axis=0, tiled=True)  68.9 us
    reshape x2, local copies, waits for them, and re-layouts, shards(): result.reshape(arrived.shape)  28.4 us
    all_to_all x1, local copies, waits for them, and re-layouts, shards(): lax.all_to_all(sendable, 'exp', split_axis=1, concat_axis=1, tiled=True)  21.2 us
    reshape x1, local copies, waits for them, and re-layouts, shards(): flat_rows = arrived.reshape(-1, features)  18.1 us
    dot_general x1, matrix products, expert_half(): jnp.dot(hidden, down_half, preferred_element_type=jnp.float32)  17.3 us
  transfers between devices with their start and end apart: 1, of which 1 were waited for; matrix products, arithmetic and copies ran while one was open for 0% of the time, Pallas kernels for 0%

commit v1 on v0

v1 whole, which is shorter than its diff:
```python
import functools

import jax
import jax.numpy as jnp
from jax import lax
from jax.experimental import pallas as pl
from jax.experimental.pallas import tpu as pltpu
from jax.sharding import PartitionSpec as P

MESH = pl.DeviceIdType.MESH
F32 = jnp.float32
BF16 = jnp.bfloat16

NY, NX, NZ = 4, 4, 8
PEERS = NY * NX
CAP = 10
ROWS = NZ * CAP
ALL = PEERS * ROWS
GATHER_AHEAD = 2
SEND_AHEAD = 2
RETURN_AHEAD = 2
GROUP = 4
SUMS = 6
ORDER = (1, 4, 3, 12, 2, 8, 5, 15, 7, 13, 6, 9, 14, 11, 10)


def kernel(
    tok, meta, w_gate, w_up, w_down, out,
    ring, metas, pick, spread, place, share, packed, came, w_in, w_out, acc, hidden, back, part, sums,
    tok_sem, meta_s, meta_r, wt_l, wt_s, wt_r, ring_s, ring_r, row_s, row_r, back_r, sum_s, sum_r,
):
    n_tok, d = tok.shape
    chunks, _, width = ring.shape
    half = w_down.shape[1]
    tiles = w_in.shape[1] // 256
    block = GROUP * ROWS
    ctx, exp = lax.axis_index("ctx"), lax.axis_index("exp")
    y, x = ctx // NX, lax.rem(ctx, NX)
    z, core = exp // 2, lax.rem(exp, 2)

    def up(j):
        return (ctx, lax.rem(z + j, NZ) * 2 + core)

    def ahead(i):
        return (lax.rem(y + i // NX, NY) * NX + lax.rem(x + i % NX, NX), exp)

    def behind(i):
        return (lax.rem(y + NY - i // NX, NY) * NX + lax.rem(x + NX - i % NX, NX), exp)

    sibling = (ctx, z * 2 + 1 - core)

    def rdma(src, dst, send, recv, to):
        return pltpu.make_async_remote_copy(
            src_ref=src, dst_ref=dst, send_sem=send, recv_sem=recv, device_id=to, device_id_type=MESH
        )

    def token_rows(j):
        return pl.ds(pl.multiple_of(j * n_tok, n_tok), n_tok)

    def peer_rows(i):
        return pl.ds(pl.multiple_of(i * ROWS, ROWS), ROWS)

    def columns(f):
        return pl.ds(pl.multiple_of(f * width, width), width)

    def own_tokens(f):
        return pltpu.make_async_copy(tok.at[:, columns(f)], ring.at[f, token_rows(0)], tok_sem.at[f])

    for f in range(chunks):
        own_tokens(f).start()
    weight_parts = (
        (w_gate.at[0], w_in, (pl.ds(0, d), 0, half)),
        (w_up.at[0], w_in, (pl.ds(0, d), 2 * half, half)),
        (w_down.at[0], w_out, (None, 0, half)),
    )

    def weight_dst(k, other):
        _, ref, (rows, at, size) = weight_parts[k]
        at = at + other * half
        if rows is None:
            return ref.at[pl.ds(at, size)]
        return ref.at[rows, pl.ds(at, size)]

    def weight_local(k):
        return pltpu.make_async_copy(weight_parts[k][0], weight_dst(k, 0), wt_l.at[k])

    def weight_remote(k):
        return rdma(weight_parts[k][0], weight_dst(k, 1), wt_s.at[k], wt_r.at[k], sibling)

    barrier = pltpu.get_barrier_semaphore()
    for j in range(1, NZ):
        pl.semaphore_signal(barrier, inc=1, device_id=up(j), device_id_type=MESH)
    for i in range(1, PEERS):
        pl.semaphore_signal(barrier, inc=1, device_id=ahead(i), device_id_type=MESH)
    pl.semaphore_signal(barrier, inc=1, device_id=sibling, device_id_type=MESH)
    metas[0] = meta[...]
    pl.semaphore_wait(barrier, NZ + PEERS - 1)

    def meta_copy(j):
        return rdma(meta, metas.at[j], meta_s.at[j], meta_r.at[j], up(NZ - j))

    def ring_copy(f, src, dst, to):
        return rdma(ring.at[f, token_rows(src)], ring.at[f, token_rows(dst)], ring_s.at[f, dst], ring_r.at[f, dst], to)

    def ring_wait(f, j):
        ring_copy(f, j, j, up(1)).wait_recv()

    def gather_start(f):
        own_tokens(f).wait()
        ring_copy(f, 0, 7, up(1)).start()
        ring_copy(f, 0, 1, up(NZ - 1)).start()

    def gather_second(f):
        ring_wait(f, 7)
        ring_copy(f, 7, 6, up(1)).start()
        ring_wait(f, 1)
        ring_copy(f, 1, 2, up(NZ - 1)).start()

    def gather_third(f):
        ring_wait(f, 6)
        ring_copy(f, 6, 5, up(1)).start()
        ring_wait(f, 2)
        ring_copy(f, 2, 3, up(NZ - 1)).start()

    def gather_fourth(f):
        odd = lax.rem(f, 2)
        ring_wait(f, 5)
        ring_wait(f, 3)
        ring_copy(f, 5 - 2 * odd, 4, up(1 + (NZ - 2) * odd)).start()

    def gather_last(f):
        ring_wait(f, 4)

    def build_places():
        for j in range(1, NZ):
            meta_copy(j).wait_recv()
        i = lax.broadcasted_iota(jnp.int32, (PEERS, n_tok), 0)
        row, col = lax.shift_right_logical(i, 2) + y, lax.bitwise_and(i, 3) + x
        owner = lax.bitwise_and(row, 3) * NX + lax.bitwise_and(col, 3)
        expert = (owner * NZ + z).astype(F32)
        earlier = (
            lax.broadcasted_iota(jnp.int32, (n_tok, n_tok), 0) < lax.broadcasted_iota(jnp.int32, (n_tok, n_tok), 1)
        ).astype(F32).astype(BF16)
        for j in range(NZ):
            named = jnp.zeros((PEERS, n_tok), F32)
            weight = jnp.zeros((PEERS, n_tok), F32)
            for k in range(8):
                hit = metas[j, k : k + 1, :] == expert
                named = named + jnp.where(hit, 1.0, 0.0)
                weight = weight + jnp.where(hit, metas[j, 8 + k : 9 + k, :], 0.0)
            rank = jnp.dot(named.astype(BF16), earlier, preferred_element_type=F32)
            place[:, j * n_tok : (j + 1) * n_tok] = jnp.where(named > 0.5, rank + float(j * CAP), -1.0)
            share[:, j * n_tok : (j + 1) * n_tok] = weight

        def one_peer(i, carry):
            slot = lax.broadcasted_iota(jnp.int32, (ROWS, NZ * n_tok), 0).astype(F32)
            hit = slot == place[pl.ds(i, 1), :]
            pick[peer_rows(i), :] = jnp.where(hit, 1.0, 0.0).astype(BF16)
            return carry

        lax.fori_loop(0, PEERS, one_peer, 0)

    def build_spread():
        lane = lax.broadcasted_iota(jnp.int32, (PEERS, ALL), 1)
        first = lax.broadcasted_iota(jnp.int32, (PEERS, ALL), 0) * ROWS
        inside = jnp.logical_and(lane >= first, lane < first + ROWS)
        widen = jnp.where(inside, 1.0, 0.0).astype(BF16)
        slot = jnp.sum(jnp.where(inside, (lane - first).astype(F32), 0.0), axis=0, keepdims=True)

        def one_block(j, carry):
            at = token_rows(j)
            dims = (((0,), (0,)), ((), ()))
            target = lax.dot_general(place[:, at].astype(BF16), widen, dims, preferred_element_type=F32)
            weight = lax.dot_general(share[:, at].astype(BF16), widen, dims, preferred_element_type=F32)
            spread[at, :] = jnp.where(target == slot, weight, 0.0).astype(BF16)
            return carry

        lax.fori_loop(0, NZ, one_block, 0)

    def pack(f):
        def one_block(b, carry):
            rows = pl.ds(pl.multiple_of(b * block, block), block)
            packed[f, rows, :] = jnp.dot(pick[rows, :], ring[f], preferred_element_type=F32).astype(BF16)
            return carry

        lax.fori_loop(0, PEERS // GROUP, one_block, 0)

    def row_copy(f, i):
        at = peer_rows(i)
        if i == 0:
            return pltpu.make_async_copy(packed.at[f, at], came.at[f, at], row_r.at[f, i])
        return rdma(packed.at[f, at], came.at[f, at], row_s.at[f, i], row_r.at[f, i], ahead(i))

    def send_rows(f):
        for i in ORDER + (0,):
            row_copy(f, i).start()

    def gate_up(f, b):
        for i in range(GROUP):
            at = peer_rows(b * GROUP + i)
            pltpu.make_async_copy(came.at[f, at], came.at[f, at], row_r.at[f, b * GROUP + i]).wait()
        rows = pl.ds(pl.multiple_of(b * block, block), block)
        depth = pl.ds(pl.multiple_of(f * width, width), width)
        xs = came[f, rows, :]
        for t in range(tiles):
            acc[t, rows, :] += jnp.dot(xs, w_in[depth, t * 256 : (t + 1) * 256], preferred_element_type=F32)

    def activate(b):
        for q in range(GROUP):
            rows = peer_rows(b * GROUP + q)
            for t in range(tiles // 2):
                g, u = acc[t, rows, :], acc[tiles // 2 + t, rows, :]
                hidden[rows, t * 256 : (t + 1) * 256] = (g / (1.0 + jnp.exp(-g)) * u).astype(BF16)

    def back_copy(n, i):
        at = peer_rows(i)
        if i == 0:
            return pltpu.make_async_copy(packed.at[n, at], back.at[n, at], back_r.at[n, i])
        return rdma(packed.at[n, at], back.at[n, at], row_s.at[n, i], back_r.at[n, i], behind(i))

    def rows_sent(n):
        for i in range(1, PEERS):
            row_copy(n, i).wait_send()

    def down(n, b):
        rows = pl.ds(pl.multiple_of(b * block, block), block)
        packed[n, rows, :] = jnp.dot(hidden[rows, :], w_out[:, columns(n)], preferred_element_type=F32).astype(BF16)

    def down_and_send(n):
        rows_sent(n)

        def one_block(b, carry):
            down(n, b)
            return carry

        lax.fori_loop(0, PEERS // GROUP, one_block, 0)
        for i in ORDER + (0,):
            back_copy(n, i).start()

    def sum_copy(n, slot, to):
        return rdma(part.at[n, token_rows(slot)], sums.at[n, token_rows(slot)], sum_s.at[n, slot], sum_r.at[n, slot], to)

    def total(n, j):
        return acc[lax.rem(n, SUMS), token_rows(j), :]

    def pass_on(n, j, slot_in, slot_out, to):
        value = total(n, j)
        if slot_in is not None:
            sum_copy(n, slot_in, to).wait_recv()
            value = value + sums[n, token_rows(slot_in), :].astype(F32)
        part[n, token_rows(slot_out), :] = value.astype(BF16)
        sum_copy(n, slot_out, to).start()

    def combine(n):
        for i in range(PEERS):
            at = peer_rows(i)
            pltpu.make_async_copy(back.at[n, at], back.at[n, at], back_r.at[n, i]).wait()

        def one_block(j, carry):
            acc[lax.rem(n, SUMS), token_rows(j), :] = jnp.dot(
                spread[token_rows(j), :], back[n], preferred_element_type=F32
            )
            return carry

        lax.fori_loop(0, NZ, one_block, 0)
        odd = lax.rem(n, 2)
        pass_on(n, 4 - odd, None, 3 - odd, up(1))
        pass_on(n, 5 - odd, None, 5 - odd, up(NZ - 1))

    def reduce_hop(n, k):
        odd = lax.rem(n, 2)
        j = 5 - k - odd
        pass_on(n, j, j, j - 1, up(1))
        j = 4 + k - odd
        pass_on(n, j, j - 1, j, up(NZ - 1))

    def reduce_fourth(n):
        odd = lax.rem(n, 2)
        pass_on(n, 1 + 6 * odd, 1 + 5 * odd, 7 * odd, up(1 + (NZ - 2) * odd))

    def reduce_last(n):
        value = total(n, 0)
        for slot in (0, 7):
            sum_copy(n, slot, up(1)).wait_recv()
            value = value + sums[n, token_rows(slot), :].astype(F32)
        out[:, columns(n)] = value.astype(BF16)

    for j in range(1, NZ):
        meta_copy(j).start()
    for f in range(GATHER_AHEAD):
        gather_start(f)
    for k in range(3):
        weight_local(k).start()
        weight_remote(k).start()

    def within(f, do):
        @pl.when(jnp.logical_and(f >= 0, f < chunks))
        def _():
            do(f)

    def out_step(t, carry):
        within(t + GATHER_AHEAD, gather_start)
        within(t, gather_second)
        within(t - 1, gather_third)
        within(t - 2, gather_fourth)

        @pl.when(t == 0)
        def _():
            acc[...] = jnp.zeros_like(acc)

        @pl.when(t == 1)
        def _():
            build_places()

        def pack_and_send(f):
            gather_last(f)
            pack(f)
            send_rows(f)

        within(t - 3, pack_and_send)

        @pl.when(t == 4)
        def _():
            build_spread()
            for k in range(3):
                weight_local(k).wait()
                weight_remote(k).wait_recv()

        def absorb(f):
            def one_block(b, carry):
                gate_up(f, b)
                return carry

            lax.fori_loop(0, PEERS // GROUP, one_block, 0)

        @pl.when(t - 3 - SEND_AHEAD >= 0)
        def _():
            absorb(t - 3 - SEND_AHEAD)

        return carry

    lax.fori_loop(0, chunks + 2 + SEND_AHEAD, out_step, 0)

    rows_sent(0)
    for b in range(PEERS // GROUP):
        gate_up(chunks - 1, b)
        activate(b)
        down(0, b)
        for i in range(b * GROUP, (b + 1) * GROUP):
            back_copy(0, i).start()
    for n in range(1, RETURN_AHEAD):
        down_and_send(n)

    def back_step(t, carry):
        within(t - 1, functools.partial(reduce_hop, k=2))
        within(t - 2, functools.partial(reduce_hop, k=3))
        within(t - 3, reduce_fourth)
        within(t - 4, reduce_last)
        within(t + RETURN_AHEAD, down_and_send)
        within(t, combine)
        return carry

    lax.fori_loop(0, chunks + 4, back_step, 0)

    for j in range(1, NZ):
        meta_copy(j).wait_send()
    for k in range(3):
        weight_remote(k).wait_send()

    def drain(n, carry):
        odd = lax.rem(n, 2)
        for j in range(1, NZ):
            ring_copy(n, j, j, up(1)).wait_send()
        for i in range(1, PEERS):
            back_copy(n, i).wait_send()
        for k in range(1, 4):
            sum_copy(n, 4 - k - odd, up(1)).wait_send()
            sum_copy(n, 4 + k - odd, up(1)).wait_send()
        sum_copy(n, 7 * odd, up(1)).wait_send()
        return carry

    lax.fori_loop(0, chunks, drain, 0)


def shards(width, tokens, expert_ids, gate_probs, w_gate, w_up, w_down):
    n_tok, d = tokens.shape
    half = w_down.shape[1]
    chunks = d // width
    weights = gate_probs / jnp.sum(gate_probs, axis=1, keepdims=True)
    meta = jnp.concatenate([expert_ids.astype(F32).T, weights.T], axis=0)
    dma = pltpu.SemaphoreType.DMA
    hbm = pl.BlockSpec(memory_space=pl.ANY)
    vmem = pl.BlockSpec(memory_space=pltpu.VMEM)
    return pl.pallas_call(
        kernel,
        out_shape=jax.ShapeDtypeStruct((n_tok, d), BF16),
        in_specs=[hbm, vmem, hbm, hbm, hbm],
        out_specs=vmem,
        scratch_shapes=[
            pltpu.VMEM((chunks, NZ * n_tok, width), BF16),
            pltpu.VMEM((NZ, 16, n_tok), F32),
            pltpu.VMEM((ALL, NZ * n_tok), BF16),
            pltpu.VMEM((NZ * n_tok, ALL), BF16),
            pltpu.VMEM((PEERS, NZ * n_tok), F32),
            pltpu.VMEM((PEERS, NZ * n_tok), F32),
            pltpu.VMEM((chunks, ALL, width), BF16),
            pltpu.VMEM((chunks, ALL, width), BF16),
            pltpu.VMEM((d, 4 * half), BF16),
            pltpu.VMEM((2 * half, d), BF16),
            pltpu.VMEM((SUMS, ALL, width), F32),
            pltpu.VMEM((ALL, 2 * half), BF16),
            pltpu.VMEM((chunks, ALL, width), BF16),
            pltpu.VMEM((chunks, NZ * n_tok, width), BF16),
            pltpu.VMEM((chunks, NZ * n_tok, width), BF16),
            dma((chunks,)),
            dma((NZ,)),
            dma((NZ,)),
            dma((3,)),
            dma((3,)),
            dma((3,)),
            dma((chunks, NZ)),
            dma((chunks, NZ)),
            dma((chunks, PEERS)),
            dma((chunks, PEERS)),
            dma((chunks, PEERS)),
            dma((chunks, NZ)),
            dma((chunks, NZ)),
        ],
        compiler_params=pltpu.CompilerParams(
            collective_id=1, has_side_effects=True, vmem_limit_bytes=60 * 1024 * 1024
        ),
        name="expert_layer",
    )(tokens, meta, w_gate, w_up, w_down)


def solution(mesh):
    return jax.shard_map(
        functools.partial(shards, 256),
        mesh=mesh,
        in_specs=(
            P(("ctx", "exp"), None),
            P(("ctx", "exp"), None),
            P(("ctx", "exp"), None),
            P(("ctx", "exp"), None, None),
            P(("ctx", "exp"), None, None),
            P(("ctx", "exp"), None, None),
        ),
        out_specs=P(("ctx", "exp"), None),
        check_vma=False,
    )
```

time: 836 us -> 189 us (0.23); the launches traced: 822 us -> 187 us
  blocking collectives: 540 us -> 0 us
  Pallas kernels: 0 us -> 183 us
  local copies, waits for them, and re-layouts: 151 us -> 1.88 us
  waiting for transfers between devices: 79.3 us -> 0 us
  matrix products: 27.3 us -> 0 us
  other arithmetic: 19.8 us -> 2.69 us
    all_to_all x3 -> x0, blocking collectives: 540 us -> none  [the longest x1 237 us: shards(): lax.all_to_all(sendable, 'exp', split_axis=1, concat_axis=1, tiled=True)]
    pallas_call x0 -> x1, Pallas kernels: none -> 183 us  [shards(): pl.pallas_call(kernel, out_shape=jax.ShapeDtypeStruct((n_tok, d), BF16),...]
    all_to_all x1 -> x0, waiting for transfers between devices: 79.3 us -> none  [shards(): lax.all_to_all(combined, 'ctx', split_axis=0, concat_axis=0, tiled=True)]
    reshape x6 -> x0, local copies, waits for them, and re-layouts: 72.6 us -> none  [the longest x2 28.4 us: shards(): result.reshape(arrived.shape)]
    all_to_all x3 -> x0, local copies, waits for them, and re-layouts: 36.8 us -> none  [the longest x1 21.2 us: shards(): lax.all_to_all(sendable, 'exp', split_axis=1, concat_axis=1, tiled=True)]
    dot_general x2 -> x0, matrix products: 27.3 us -> none  [the longest x1 17.3 us: expert_half(): jnp.dot(hidden, down_half, preferred_element_type=jnp.float32)]
    reduce_sum x3 -> x0, other arithmetic: 18.7 us -> none  [the longest x1 11.1 us: shards(): jnp.sum(returned.reshape(ctx_size, groups, 2, capacity, features).astype(...]
    gather x2 -> x0, local copies, waits for them, and re-layouts: 18.4 us -> none  [the longest x1 12.1 us: shards(): picked = homebound[places].reshape(tok_rows, chosen, features)]
  transfers between devices with their start and end apart: 1 -> 0, of which waited for: 1 -> 0; matrix products, arithmetic and copies ran while one was open for 0% -> 0% of each run, Pallas kernels for 0% -> 0%
where the time goes in v1:
time: 189 us; the launch traced here: 187 us
  Pallas kernels  183 us (97%)
  other arithmetic  2.69 us (1%)
    pallas_call x1, Pallas kernels, shards(): pl.pallas_call(kernel, out_shape=jax.ShapeDtypeStruct((n_tok, d), BF16),...  183 us

profile of v1, /device:TPU:32, one launch (start us, length us, event | category | flops | bytes accessed | tf_op | source)
XLA Modules:
  0.0 187.3 jit_solution(3387462411667683587)
XLA Ops:
  0.0 0.7 reduce_sum.9
  0.7 0.7 divide_bitcast_fusion
  1.4 0.7 convert_bitcast_fusion
  2.1 0.6 pad_maximum_fusion.meta
  2.7 182.7 %expert_layer.1 = bf16[128,2048]{1,0:T(8,128)(2,1)} custom-call(bf16[128,2048]{1,0:T(8,128)(2,1)} %tok.1, f32[16,128]{1,0:T(8,128)} %pad_maximum_fusion.meta, bf16[1,2048,384]{2,1,0:T(8,128)(2,1)} %w_gate.1, bf16[1,2048,384]{2,1,0:T(8,128)(2,1)} %w_up.1, bf16[1,384,2048]{2,1,0:T(8,128)(2,1)} %w_down.1), custom_call_target="tpu_custom_call" | custom-call | tf_op jit(solution)/shard_map/expert_layer/pallas_call | solution.py:394
  185.4 1.9 %copy.8 = bf16[128,2048]{1,0:T(8,128)(2,1)} copy(bf16[128,2048]{1,0:T(8,128)(2,1)} %expert_layer.1) | data formatting | bytes 1048576

commit v2 on v1

--- a/solution.py
+++ b/solution.py
@@ -16,7 +16,7 @@
 CAP = 10
 ROWS = NZ * CAP
 ALL = PEERS * ROWS
-GATHER_AHEAD = 2
+GATHER_AHEAD = 1
 SEND_AHEAD = 2
 RETURN_AHEAD = 2
 GROUP = 4
@@ -25,12 +25,12 @@
 
 
 def kernel(
-    tok, meta, w_gate, w_up, w_down, out,
+    tok, ids, probs, w_gate, w_up, w_down, out,
     ring, metas, pick, spread, place, share, packed, came, w_in, w_out, acc, hidden, back, part, sums,
     tok_sem, meta_s, meta_r, wt_l, wt_s, wt_r, ring_s, ring_r, row_s, row_r, back_r, sum_s, sum_r,
 ):
     n_tok, d = tok.shape
-    chunks, _, width = ring.shape
+    chunks, _, _, width = ring.shape
     half = w_down.shape[1]
     tiles = w_in.shape[1] // 256
     block = GROUP * ROWS
@@ -60,11 +60,17 @@
     def peer_rows(i):
         return pl.ds(pl.multiple_of(i * ROWS, ROWS), ROWS)
 
+    def peers(b):
+        return pl.ds(pl.multiple_of(b * GROUP, GROUP), GROUP)
+
+    def flat(value):
+        return value.reshape(value.shape[0] * value.shape[1], value.shape[2])
+
     def columns(f):
         return pl.ds(pl.multiple_of(f * width, width), width)
 
     def own_tokens(f):
-        return pltpu.make_async_copy(tok.at[:, columns(f)], ring.at[f, token_rows(0)], tok_sem.at[f])
+        return pltpu.make_async_copy(tok.at[:, columns(f)], ring.at[f, 0], tok_sem.at[f])
 
     for f in range(chunks):
         own_tokens(f).start()
@@ -93,14 +99,20 @@
     for i in range(1, PEERS):
         pl.semaphore_signal(barrier, inc=1, device_id=ahead(i), device_id_type=MESH)
     pl.semaphore_signal(barrier, inc=1, device_id=sibling, device_id_type=MESH)
-    metas[0] = meta[...]
+    weights = probs[...] / jnp.sum(probs[...], axis=1, keepdims=True)
+    same = lax.broadcasted_iota(jnp.int32, (n_tok, n_tok), 0) == lax.broadcasted_iota(jnp.int32, (n_tok, n_tok), 1)
+    eye = jnp.where(same, 1.0, 0.0).astype(BF16)
+    turn = (((0,), (0,)), ((), ()))
+    metas[0, 0:8] = lax.dot_general(ids[...].astype(F32).astype(BF16), eye, turn, preferred_element_type=F32)
+    metas[0, 8:16] = lax.dot_general(weights.astype(BF16), eye, turn, preferred_element_type=F32)
+    acc[...] = jnp.zeros_like(acc)
     pl.semaphore_wait(barrier, NZ + PEERS - 1)
 
     def meta_copy(j):
-        return rdma(meta, metas.at[j], meta_s.at[j], meta_r.at[j], up(NZ - j))
+        return rdma(metas.at[0], metas.at[j], meta_s.at[j], meta_r.at[j], up(NZ - j))
 
     def ring_copy(f, src, dst, to):
-        return rdma(ring.at[f, token_rows(src)], ring.at[f, token_rows(dst)], ring_s.at[f, dst], ring_r.at[f, dst], to)
+        return rdma(ring.at[f, src], ring.at[f, dst], ring_s.at[f, dst], ring_r.at[f, dst], to)
 
     def ring_wait(f, j):
         ring_copy(f, j, j, up(1)).wait_recv()
@@ -123,7 +135,7 @@
         ring_copy(f, 2, 3, up(NZ - 1)).start()
 
     def gather_fourth(f):
-        odd = lax.rem(f, 2)
+        odd = lax.rem(f + core, 2)
         ring_wait(f, 5)
         ring_wait(f, 3)
         ring_copy(f, 5 - 2 * odd, 4, up(1 + (NZ - 2) * odd)).start()
@@ -180,16 +192,16 @@
     def pack(f):
         def one_block(b, carry):
             rows = pl.ds(pl.multiple_of(b * block, block), block)
-            packed[f, rows, :] = jnp.dot(pick[rows, :], ring[f], preferred_element_type=F32).astype(BF16)
+            value = jnp.dot(pick[rows, :], flat(ring[f]), preferred_element_type=F32).astype(BF16)
+            packed[f, peers(b)] = value.reshape(GROUP, ROWS, width)
             return carry
 
         lax.fori_loop(0, PEERS // GROUP, one_block, 0)
 
     def row_copy(f, i):
-        at = peer_rows(i)
         if i == 0:
-            return pltpu.make_async_copy(packed.at[f, at], came.at[f, at], row_r.at[f, i])
-        return rdma(packed.at[f, at], came.at[f, at], row_s.at[f, i], row_r.at[f, i], ahead(i))
+            return pltpu.make_async_copy(packed.at[f, i], came.at[f, i], row_r.at[f, i])
+        return rdma(packed.at[f, i], came.at[f, i], row_s.at[f, i], row_r.at[f, i], ahead(i))
 
     def send_rows(f):
         for i in ORDER + (0,):
@@ -197,11 +209,11 @@
 
     def gate_up(f, b):
         for i in range(GROUP):
-            at = peer_rows(b * GROUP + i)
-            pltpu.make_async_copy(came.at[f, at], came.at[f, at], row_r.at[f, b * GROUP + i]).wait()
+            at = b * GROUP + i
+            pltpu.make_async_copy(came.at[f, at], came.at[f, at], row_r.at[f, at]).wait()
         rows = pl.ds(pl.multiple_of(b * block, block), block)
         depth = pl.ds(pl.multiple_of(f * width, width), width)
-        xs = came[f, rows, :]
+        xs = flat(came[f, peers(b)])
         for t in range(tiles):
             acc[t, rows, :] += jnp.dot(xs, w_in[depth, t * 256 : (t + 1) * 256], preferred_element_type=F32)
 
@@ -210,13 +222,12 @@
             rows = peer_rows(b * GROUP + q)
             for t in range(tiles // 2):
                 g, u = acc[t, rows, :], acc[tiles // 2 + t, rows, :]
-                hidden[rows, t * 256 : (t + 1) * 256] = (g / (1.0 + jnp.exp(-g)) * u).astype(BF16)
+                hidden[rows, t * 256 : (t + 1) * 256] = (g * (0.5 + 0.5 * jnp.tanh(0.5 * g)) * u).astype(BF16)
 
     def back_copy(n, i):
-        at = peer_rows(i)
         if i == 0:
-            return pltpu.make_async_copy(packed.at[n, at], back.at[n, at], back_r.at[n, i])
-        return rdma(packed.at[n, at], back.at[n, at], row_s.at[n, i], back_r.at[n, i], behind(i))
+            return pltpu.make_async_copy(packed.at[n, i], back.at[n, i], back_r.at[n, i])
+        return rdma(packed.at[n, i], back.at[n, i], row_s.at[n, i], back_r.at[n, i], behind(i))
 
     def rows_sent(n):
         for i in range(1, PEERS):
@@ -224,7 +235,8 @@
 
     def down(n, b):
         rows = pl.ds(pl.multiple_of(b * block, block), block)
-        packed[n, rows, :] = jnp.dot(hidden[rows, :], w_out[:, columns(n)], preferred_element_type=F32).astype(BF16)
+        value = jnp.dot(hidden[rows, :], w_out[:, columns(n)], preferred_element_type=F32).astype(BF16)
+        packed[n, peers(b)] = value.reshape(GROUP, ROWS, width)
 
     def down_and_send(n):
         rows_sent(n)
@@ -238,7 +250,7 @@
             back_copy(n, i).start()
 
     def sum_copy(n, slot, to):
-        return rdma(part.at[n, token_rows(slot)], sums.at[n, token_rows(slot)], sum_s.at[n, slot], sum_r.at[n, slot], to)
+        return rdma(part.at[n, slot], sums.at[n, slot], sum_s.at[n, slot], sum_r.at[n, slot], to)
 
     def total(n, j):
         return acc[lax.rem(n, SUMS), token_rows(j), :]
@@ -247,47 +259,47 @@
         value = total(n, j)
         if slot_in is not None:
             sum_copy(n, slot_in, to).wait_recv()
-            value = value + sums[n, token_rows(slot_in), :].astype(F32)
-        part[n, token_rows(slot_out), :] = value.astype(BF16)
+            value = value + sums[n, slot_in].astype(F32)
+        part[n, slot_out] = value.astype(BF16)
         sum_copy(n, slot_out, to).start()
 
     def combine(n):
         for i in range(PEERS):
-            at = peer_rows(i)
-            pltpu.make_async_copy(back.at[n, at], back.at[n, at], back_r.at[n, i]).wait()
+            pltpu.make_async_copy(back.at[n, i], back.at[n, i], back_r.at[n, i]).wait()
 
         def one_block(j, carry):
             acc[lax.rem(n, SUMS), token_rows(j), :] = jnp.dot(
-                spread[token_rows(j), :], back[n], preferred_element_type=F32
+                spread[token_rows(j), :], flat(back[n]), preferred_element_type=F32
             )
             return carry
 
         lax.fori_loop(0, NZ, one_block, 0)
-        odd = lax.rem(n, 2)
+        odd = lax.rem(n + core, 2)
         pass_on(n, 4 - odd, None, 3 - odd, up(1))
         pass_on(n, 5 - odd, None, 5 - odd, up(NZ - 1))
 
     def reduce_hop(n, k):
-        odd = lax.rem(n, 2)
+        odd = lax.rem(n + core, 2)
         j = 5 - k - odd
         pass_on(n, j, j, j - 1, up(1))
         j = 4 + k - odd
         pass_on(n, j, j - 1, j, up(NZ - 1))
 
     def reduce_fourth(n):
-        odd = lax.rem(n, 2)
+        odd = lax.rem(n + core, 2)
         pass_on(n, 1 + 6 * odd, 1 + 5 * odd, 7 * odd, up(1 + (NZ - 2) * odd))
 
     def reduce_last(n):
         value = total(n, 0)
         for slot in (0, 7):
             sum_copy(n, slot, up(1)).wait_recv()
-            value = value + sums[n, token_rows(slot), :].astype(F32)
+            value = value + sums[n, slot].astype(F32)
         out[:, columns(n)] = value.astype(BF16)
 
+    gather_start(0)
     for j in range(1, NZ):
         meta_copy(j).start()
-    for f in range(GATHER_AHEAD):
+    for f in range(1, GATHER_AHEAD):
         gather_start(f)
     for k in range(3):
         weight_local(k).start()
@@ -303,10 +315,6 @@
         within(t, gather_second)
         within(t - 1, gather_third)
         within(t - 2, gather_fourth)
-
-        @pl.when(t == 0)
-        def _():
-            acc[...] = jnp.zeros_like(acc)
 
         @pl.when(t == 1)
         def _():
@@ -352,12 +360,12 @@
         down_and_send(n)
 
     def back_step(t, carry):
+        within(t - 4, reduce_last)
+        within(t - 3, reduce_fourth)
+        within(t - 2, functools.partial(reduce_hop, k=3))
         within(t - 1, functools.partial(reduce_hop, k=2))
-        within(t - 2, functools.partial(reduce_hop, k=3))
-        within(t - 3, reduce_fourth)
-        within(t - 4, reduce_last)
+        within(t, combine)
         within(t + RETURN_AHEAD, down_and_send)
-        within(t, combine)
         return carry
 
     lax.fori_loop(0, chunks + 4, back_step, 0)
@@ -368,7 +376,7 @@
         weight_remote(k).wait_send()
 
     def drain(n, carry):
-        odd = lax.rem(n, 2)
+        odd = lax.rem(n + core, 2)
         for j in range(1, NZ):
             ring_copy(n, j, j, up(1)).wait_send()
         for i in range(1, PEERS):
@@ -386,32 +394,30 @@
     n_tok, d = tokens.shape
     half = w_down.shape[1]
     chunks = d // width
-    weights = gate_probs / jnp.sum(gate_probs, axis=1, keepdims=True)
-    meta = jnp.concatenate([expert_ids.astype(F32).T, weights.T], axis=0)
     dma = pltpu.SemaphoreType.DMA
     hbm = pl.BlockSpec(memory_space=pl.ANY)
     vmem = pl.BlockSpec(memory_space=pltpu.VMEM)
     return pl.pallas_call(
         kernel,
         out_shape=jax.ShapeDtypeStruct((n_tok, d), BF16),
-        in_specs=[hbm, vmem, hbm, hbm, hbm],
+        in_specs=[hbm, vmem, vmem, hbm, hbm, hbm],
         out_specs=vmem,
         scratch_shapes=[
-            pltpu.VMEM((chunks, NZ * n_tok, width), BF16),
+            pltpu.VMEM((chunks, NZ, n_tok, width), BF16),
             pltpu.VMEM((NZ, 16, n_tok), F32),
             pltpu.VMEM((ALL, NZ * n_tok), BF16),
             pltpu.VMEM((NZ * n_tok, ALL), BF16),
             pltpu.VMEM((PEERS, NZ * n_tok), F32),
             pltpu.VMEM((PEERS, NZ * n_tok), F32),
-            pltpu.VMEM((chunks, ALL, width), BF16),
-            pltpu.VMEM((chunks, ALL, width), BF16),
+            pltpu.VMEM((chunks, PEERS, ROWS, width), BF16),
+            pltpu.VMEM((chunks, PEERS, ROWS, width), BF16),
             pltpu.VMEM((d, 4 * half), BF16),
             pltpu.VMEM((2 * half, d), BF16),
             pltpu.VMEM((SUMS, ALL, width), F32),
             pltpu.VMEM((ALL, 2 * half), BF16),
-            pltpu.VMEM((chunks, ALL, width), BF16),
-            pltpu.VMEM((chunks, NZ * n_tok, width), BF16),
-            pltpu.VMEM((chunks, NZ * n_tok, width), BF16),
+            pltpu.VMEM((chunks, PEERS, ROWS, width), BF16),
+            pltpu.VMEM((chunks, NZ, n_tok, width), BF16),
+            pltpu.VMEM((chunks, NZ, n_tok, width), BF16),
             dma((chunks,)),
             dma((NZ,)),
             dma((NZ,)),
@@ -430,7 +436,7 @@
             collective_id=1, has_side_effects=True, vmem_limit_bytes=60 * 1024 * 1024
         ),
         name="expert_layer",
-    )(tokens, meta, w_gate, w_up, w_down)
+    )(tokens, expert_ids, gate_probs, w_gate, w_up, w_down)
 
 
 def solution(mesh):

time: 189 us -> 185 us (0.979)
  Pallas kernels: 183 us -> 179 us
  local copies, waits for them, and re-layouts: 1.88 us -> 4.7 us
  other arithmetic: 2.69 us -> 0 us
    pallas_call x1, Pallas kernels: 183 us -> 179 us  [shards(): pl.pallas_call(kernel, out_shape=jax.ShapeDtypeStruct((n_tok, d), BF16),...]
    unnamed x1 -> x3, local copies, waits for them, and re-layouts: 1.88 us -> 4.7 us
where the time goes in v2:
time: 185 us; the launch traced here: 184 us
  Pallas kernels  179 us (97%)
  local copies, waits for them, and re-layouts  4.7 us (3%)
    pallas_call x1, Pallas kernels, shards(): pl.pallas_call(kernel, out_shape=jax.ShapeDtypeStruct((n_tok, d), BF16),...  179 us
    unnamed x3, local copies, waits for them, and re-layouts  4.7 us

profile of v2, /device:TPU:32, one launch (start us, length us, event | category | flops | bytes accessed | tf_op | source)
XLA Modules:
  0.0 183.6 jit_solution(13126637948050292609)
XLA Ops:
  0.0 1.4 copy.7.ids
  1.4 1.4 copy.8.probs
  2.8 178.8 %expert_layer.1 = bf16[128,2048]{1,0:T(8,128)(2,1)} custom-call(bf16[128,2048]{1,0:T(8,128)(2,1)} %tok.1, s32[128,8]{1,0:T(8,128)} %copy.7.ids, f32[128,8]{1,0:T(8,128)} %copy.8.probs, bf16[1,2048,384]{2,1,0:T(8,128)(2,1)} %w_gate.1, bf16[1,2048,384]{2,1,0:T(8,128)(2,1)} %w_up.1, bf16[1,384,2048]{2,1,0:T(8,128)(2,1)} %w_down.1), custom_call_target="tpu_custom_call" | custom-call | tf_op jit(solution)/shard_map/expert_layer/pallas_call | solution.py:400
  181.7 1.9 %copy.10 = bf16[128,2048]{1,0:T(8,128)(2,1)} copy(bf16[128,2048]{1,0:T(8,128)(2,1)} %expert_layer.1) | data formatting | bytes 1048576

commit v3 on v2

--- a/solution.py
+++ b/solution.py
@@ -99,12 +99,8 @@
     for i in range(1, PEERS):
         pl.semaphore_signal(barrier, inc=1, device_id=ahead(i), device_id_type=MESH)
     pl.semaphore_signal(barrier, inc=1, device_id=sibling, device_id_type=MESH)
-    weights = probs[...] / jnp.sum(probs[...], axis=1, keepdims=True)
-    same = lax.broadcasted_iota(jnp.int32, (n_tok, n_tok), 0) == lax.broadcasted_iota(jnp.int32, (n_tok, n_tok), 1)
-    eye = jnp.where(same, 1.0, 0.0).astype(BF16)
-    turn = (((0,), (0,)), ((), ()))
-    metas[0, 0:8] = lax.dot_general(ids[...].astype(F32).astype(BF16), eye, turn, preferred_element_type=F32)
-    metas[0, 8:16] = lax.dot_general(weights.astype(BF16), eye, turn, preferred_element_type=F32)
+    metas[0, 0:8] = ids[...].astype(F32)
+    metas[0, 8:16] = probs[...] / jnp.sum(probs[...], axis=0, keepdims=True)
     acc[...] = jnp.zeros_like(acc)
     pl.semaphore_wait(barrier, NZ + PEERS - 1)
 
@@ -436,7 +432,7 @@
             collective_id=1, has_side_effects=True, vmem_limit_bytes=60 * 1024 * 1024
         ),
         name="expert_layer",
-    )(tokens, expert_ids, gate_probs, w_gate, w_up, w_down)
+    )(tokens, expert_ids.T, gate_probs.T, w_gate, w_up, w_down)
 
 
 def solution(mesh):

time: 185 us -> 181 us (0.978)
  local copies, waits for them, and re-layouts: 4.7 us -> 1.88 us
    unnamed x3 -> x1, local copies, waits for them, and re-layouts: 4.7 us -> 1.88 us
where the time goes in v3:
time: 181 us
  Pallas kernels  179 us (99%)
  local copies, waits for them, and re-layouts  1.88 us (1%)
    pallas_call x1, Pallas kernels, shards(): pl.pallas_call(kernel, out_shape=jax.ShapeDtypeStruct((n_tok, d), BF16),...  179 us

profile of v3, /device:TPU:32, one launch (start us, length us, event | category | flops | bytes accessed | tf_op | source)
XLA Modules:
  0.0 181.2 jit_solution(11367325850032427971)
XLA Ops:
  0.0 179.3 %expert_layer.1 = bf16[128,2048]{1,0:T(8,128)(2,1)} custom-call(bf16[128,2048]{1,0:T(8,128)(2,1)} %tok.1, s32[8,128]{1,0:T(8,128)} %bitcast.2, f32[8,128]{1,0:T(8,128)} %bitcast.3, bf16[1,2048,384]{2,1,0:T(8,128)(2,1)} %w_gate.1, bf16[1,2048,384]{2,1,0:T(8,128)(2,1)} %w_up.1, bf16[1,384,2048]{2,1,0:T(8,128)(2,1)} %w_down.1), custom_call_target="tpu_custom_call" | custom-call | tf_op jit(solution)/shard_map/expert_layer/pallas_call | solution.py:396
  179.3 1.9 %copy.8 = bf16[128,2048]{1,0:T(8,128)(2,1)} copy(bf16[128,2048]{1,0:T(8,128)(2,1)} %expert_layer.1) | data formatting | bytes 1048576

commit v4 on v3

--- a/solution.py
+++ b/solution.py
@@ -297,9 +297,6 @@
         meta_copy(j).start()
     for f in range(1, GATHER_AHEAD):
         gather_start(f)
-    for k in range(3):
-        weight_local(k).start()
-        weight_remote(k).start()
 
     def within(f, do):
         @pl.when(jnp.logical_and(f >= 0, f < chunks))
@@ -321,9 +318,15 @@
             pack(f)
             send_rows(f)
 
+            @pl.when(f == 0)
+            def _():
+                for k in range(3):
+                    weight_local(k).start()
+                    weight_remote(k).start()
+
         within(t - 3, pack_and_send)
 
-        @pl.when(t == 4)
+        @pl.when(t == 5)
         def _():
             build_spread()
             for k in range(3):

time: 181 us -> 181 us (level)
  no operation moved by 1% of the time
where the time goes in v4:
time: 181 us; the launch traced here: 180 us
  Pallas kernels  178 us (98%)
  local copies, waits for them, and re-layouts  1.88 us (1%)
    pallas_call x1, Pallas kernels, shards(): pl.pallas_call(kernel, out_shape=jax.ShapeDtypeStruct((n_tok, d), BF16),...  178 us

profile of v4, /device:TPU:32, one launch (start us, length us, event | category | flops | bytes accessed | tf_op | source)
XLA Modules:
  0.0 179.8 jit_solution(12220906015415706551)
XLA Ops:
  0.0 177.9 %expert_layer.1 = bf16[128,2048]{1,0:T(8,128)(2,1)} custom-call(bf16[128,2048]{1,0:T(8,128)(2,1)} %tok.1, s32[8,128]{1,0:T(8,128)} %bitcast.2, f32[8,128]{1,0:T(8,128)} %bitcast.3, bf16[1,2048,384]{2,1,0:T(8,128)(2,1)} %w_gate.1, bf16[1,2048,384]{2,1,0:T(8,128)(2,1)} %w_up.1, bf16[1,384,2048]{2,1,0:T(8,128)(2,1)} %w_down.1), custom_call_target="tpu_custom_call" | custom-call | tf_op jit(solution)/shard_map/expert_layer/pallas_call | solution.py:399
  177.9 1.9 %copy.8 = bf16[128,2048]{1,0:T(8,128)(2,1)} copy(bf16[128,2048]{1,0:T(8,128)(2,1)} %expert_layer.1) | data formatting | bytes 1048576
